TPU v7x, 256 devices: a whole 4x4x8 slice. The times are simulated.
256 devices in a mesh: dp: 16 (over z, core), section: 16 (over x, y).
Axes of the slice: x: 4, y: 4, z: 8, core: 2. Of those that a mesh axis runs over, the one named last changes fastest.
Arguments:
- layer_inputs: bfloat16 [16, 16, 512, 2048], P('section', 'dp'), may hold values from -24 to 24
- output_grads: bfloat16 [16, 16, 512, 4608], P('section', 'dp'), may hold values from -5.0351435e-05 to 5.0351435e-05
- lengths: int32 [16], P('dp'), may hold values from 1 to 512, as said below
Outputs:
- clipped_grad: bfloat16 [16, 2048, 4608], P('section', 'dp')
Inputs may be any that keep to these rules, and one draw needn't show every extreme that they name: `lengths`: some example has all 512 tokens live.
All inputs are finite; a program needn't handle non-finite values.
Results may differ from a plain program's by a relative error of at most 0.024.
Values may be sent and summed in bfloat16 or wider, within the bound.
A program may use at most 128 MiB of HBM per device.

v0:
```python
import math

import jax
import jax.numpy as jnp
from jax import lax
from jax.sharding import PartitionSpec as P


def gram_norm(pair):
    inputs, grads = pair
    gram_in = jnp.dot(inputs, inputs.T, preferred_element_type=jnp.float32)
    gram_out = jnp.dot(grads, grads.T, preferred_element_type=jnp.float32)
    return jnp.sum(gram_in * gram_out)


def shards(layer_inputs, output_grads, lengths):
    inputs = layer_inputs[0]
    grads = output_grads[0]
    seq_len = inputs.shape[1]
    positions = jnp.arange(seq_len, dtype=jnp.int32)
    live = positions[None, :] < lengths[:, None]
    masked = jnp.where(live[:, :, None], grads, jnp.zeros_like(grads))
    partial_norms = lax.map(gram_norm, (inputs, masked))
    total = lax.psum(partial_norms, "section")
    factor = jnp.minimum(1.0, 1.0 / jnp.sqrt(total + 1e-06))
    width_in = inputs.shape[2]
    width_out = grads.shape[2]
    examples = inputs.shape[0] * lax.axis_size("dp")
    weight = math.sqrt(width_in * width_out * lax.axis_size("section") / examples)
    scaled = (factor[:, None, None] * masked.astype(jnp.float32)).astype(jnp.bfloat16)
    flat_in = inputs.reshape(-1, width_in)
    flat_out = scaled.reshape(-1, width_out)
    term = lax.dot_general(
        flat_in, flat_out, (((0,), (0,)), ((), ())), preferred_element_type=jnp.float32
    )
    summed = lax.psum_scatter(
        term.astype(jnp.bfloat16), "dp", scatter_dimension=0, tiled=True
    ).astype(jnp.float32)
    return (summed * weight).astype(jnp.bfloat16)[None]


def solution(mesh):
    placed = (P("section", "dp", None, None), P("section", "dp", None, None), P("dp"))
    return jax.shard_map(
        shards, mesh=mesh, in_specs=placed, out_specs=P("section", "dp", None), check_vma=False
    )
```

profile of v0, /device:TPU:1, one launch (start us, length us, event | category | flops | bytes accessed | tf_op | source)
XLA Modules:
  0.0 219.5 jit_solution(10684724968510147787)
XLA Ops:
  6.5 0.0 copy-start
  6.5 0.0 reduce-scatter.4.cloned.1.call-start
  7.4 6.5 %fusion.3 = f32[512,512]{1,0:T(8,128)S(1)} fusion(bf16[1,1,512,4608]{3,2,1,0:T(8,128)(2,1)} %param.4, pred[512]{0:T(512)(128)(4,1)S(1)} %iota_compare_fusion), kind=kOutput, calls=%fused_computation.4 | convolution fusion | flops 2418278400 | bytes 5767680 | tf_op jit(solution)/shard_map/while/body/eval_jaxpr/dot_general | solution.py:12
  13.8 0.0 copy-done
  13.9 2.0 fusion.13
  15.9 34.9 %psum.7 = f32[1]{0:T(128)} all-reduce(f32[1]{0:T(128)} %bitcast.4), channel_id=1, replica_groups=mesh['dp'=16,'section'=16] {'section'}, use_global_device_ids=true, to_apply=%region_1.2 | all-reduce | flops 1 | bytes 8 | tf_op jit(solution)/shard_map/psum | solution.py:24
  51.4 15.9 %fusion = bf16[2048,4608]{0,1:T(8,128)(2,1)} fusion(f32[]{:T(128)} %bitcast.5, bf16[1,1,512,4608]{3,2,1,0:T(8,128)(2,1)} %param.4, pred[512]{0:T(512)(128)(4,1)S(1)} %iota_compare_fusion, bf16[1,1,512,2048]{3,2,1,0:T(8,128)(2,1)S(1)} %copy-done), kind=kOutput, calls=%fused_computation.1 | convolution fusion | flops 9682550784 | bytes 25690628 | tf_op jit(solution)/shard_map/dot_general | solution.py:33
  67.4 24.7 %copy.6 = bf16[2048,4608]{1,0:T(8,128)(2,1)} copy(bf16[2048,4608]{0,1:T(8,128)(2,1)} %fusion) | data formatting | bytes 37748736
  92.0 0.0 reduce-scatter.4.cloned.1.call-update
  92.1 115.3 %reduce-scatter.4.cloned.1.call-done = bf16[128,4608]{1,0:T(8,128)(2,1)} async-done(((bf16[2048,4608]{1,0:T(8,128)(2,1)}), bf16[128,4608]{1,0:T(8,128)(2,1)}) %reduce-scatter.4.cloned.1.call-update) | async-done | bytes 1179664
  207.4 1.7 copy.7
  209.1 1.2 fusion.12
  210.3 2.4 %copy.5 = bf16[1,128,4608]{2,1,0:T(8,128)(2,1)} copy(bf16[1,128,4608]{1,2,0:T(8,128)(2,1)} %fusion.12) | data formatting | bytes 2359296 | tf_op jit(solution)/shard_map/broadcast_in_dim | solution.py:39
  (1 shorter events, 0.0 us)
Async XLA Ops:
  6.5 7.3 %copy-start = (bf16[1,1,512,2048]{3,2,1,0:T(8,128)(2,1)S(1)}, bf16[1,1,512,2048]{3,2,1,0:T(8,128)(2,1)}, u32[]{:S(2)}) copy-start(bf16[1,1,512,2048]{3,2,1,0:T(8,128)(2,1)} %param.3) | copy-start | bytes 6291460
  6.5 200.8 %reduce-scatter.4.cloned.1.call-start = ((), (), s32[]{:S(2)}) async-start(), calls=%async_computation.1 | async-start | bytes 20054016
Sparse Core Ops, SparseCore 0:
  92.2 115.1 reduce-scatter.3
where the time goes:
time: 221 us; the launch traced here: 220 us
  waiting for transfers between devices  115 us (52%)
  blocking collectives  34.9 us (16%)
  local copies, waits for them, and re-layouts  28.7 us (13%)
  matrix products  24.4 us (11%)
  between operations  14.9 us (7%)
    unnamed x2, waiting for transfers between devices  115 us
    psum x1, blocking collectives, shards(): total = lax.psum(partial_norms, 'section')  34.9 us
    unnamed x4, local copies, waits for them, and re-layouts  26.4 us
    dot_general x1, matrix products, shards(): lax.dot_general(flat_in, flat_out, (((0,), (0,)), ((), ())), preferred_el...  15.9 us
    dot_general x1, matrix products, gram_norm(): gram_out = jnp.dot(grads, grads.T, preferred_element_type=jnp.float32)  6.49 us
  transfers between devices with their start and end apart: 1, of which 1 were waited for; matrix products, arithmetic and copies ran while one was open for 0% of the time, Pallas kernels for 0%

commit v1 on v0

v1 whole, which is shorter than its diff:
```python
import functools
import math

import jax
import jax.numpy as jnp
from jax import lax
from jax.experimental import pallas as pl
from jax.experimental.pallas import tpu as pltpu
from jax.sharding import PartitionSpec as P

F32 = jnp.float32
BF16 = jnp.bfloat16
MESH = pl.DeviceIdType.MESH
PIECES = 3


def kernel(dims, weight, len_ref, x_ref, g_ref, out_ref, xv, xb, gv, xt, sendb, recvb, fin, gin, gout, tile, norms, lens,
           facs, xe, sendu, recvu, upfac, pre, xe_sem, early_send, early_recv, up_send, up_recv, xv_sem, xb_sem, gv_sem, xb_send, gv_send, len_sem, norm_send, norm_recv, fac_sem, ring_send, ring_recv):
    n_chips, n_sec, rows = dims
    seq = x_ref.shape[0]
    width = gv.shape[2]
    chunks = 2 * PIECES
    half = seq // 2
    steps = n_chips - 1
    dp = lax.axis_index("dp")
    sec = lax.axis_index("section")
    z = lax.div(dp, 2)
    core = lax.rem(dp, 2)
    partner = dp + 1 - 2 * core
    ahead = lax.rem(dp + 2, 2 * n_chips)
    behind = lax.rem(dp + 2 * n_chips - 2, 2 * n_chips)
    ring_to = (ahead, behind)

    xe_cols = pl.ds(pl.multiple_of(lax.rem(z + n_chips // 2, n_chips) * 2 * rows, 128), 2 * rows)
    xe_copy = pltpu.make_async_copy(x_ref.at[:, xe_cols], xe, xe_sem)
    xe_copy.start()
    x_copy = pltpu.make_async_copy(x_ref, xv, xv_sem)

    def g_copy(c):
        cols = pl.ds(pl.multiple_of(c * width, 128), width)
        return pltpu.make_async_copy(g_ref.at[:, cols], gv.at[c, pl.ds(0, seq)], gv_sem.at[0, c])

    def g_swap(c):
        cols = pl.ds(pl.multiple_of(c * width, 128), width)
        return pltpu.make_async_remote_copy(
            g_ref.at[:, cols], gv.at[c, pl.ds(seq, seq)], gv_send.at[c], gv_sem.at[1, c],
            device_id=(partner, sec), device_id_type=MESH)

    def owner(k):
        far = lax.div(k + 1, 2)
        turn = jnp.where(lax.rem(k, 2) == 1, n_chips - far, far)
        return lax.rem(z + n_chips // 2 + turn, n_chips)

    def x_cols(k, c):
        return pl.ds(pl.multiple_of((2 * k + c) * rows, 128), rows)

    def xb_copy(k):
        return pltpu.make_async_copy(x_ref.at[:, x_cols(k, core)], xb.at[0, k], xb_sem.at[0, k])

    def xb_swap(k):
        return pltpu.make_async_remote_copy(
            x_ref.at[:, x_cols(k, 1 - core)], xb.at[1, k], xb_send.at[k], xb_sem.at[1, k],
            device_id=(partner, sec), device_id_type=MESH)

    for d in range(2):
        g_copy(d * PIECES).start()
    x_copy.start()

    barrier = pltpu.get_barrier_semaphore()
    for peer in (partner, ahead, behind, ahead + partner - dp, behind + partner - dp):
        pl.semaphore_signal(barrier, inc=1, device_id=(peer, sec), device_id_type=MESH)

    @pl.loop(1, n_sec)
    def _(j):
        pl.semaphore_signal(barrier, inc=1, device_id=(dp, lax.rem(sec + j, n_sec)), device_id_type=MESH)

    @pl.loop(1, PIECES)
    def _(s):
        for d in range(2):
            g_copy(d * PIECES + s).start()

    @pl.loop(0, n_chips)
    def _(k):
        xb_copy(owner(k)).start()

    lens[0] = jnp.full(lens.shape[1:], len_ref[0], F32)

    xe_copy.wait()
    token = lax.broadcasted_iota(jnp.int32, xe.shape, 0)
    xet = jnp.where(token < len_ref[0], xe[...].astype(F32), 0.0).T.astype(BF16)
    for d in range(2):
        g_copy(d * PIECES).wait()
        early = jnp.dot(xet, gv[d * PIECES, :seq], preferred_element_type=F32).astype(BF16)
        for e in range(2):
            sendu[d, e] = early[e * rows:(e + 1) * rows]

    def early_copy(d, e):
        slot = lax.rem(core + e, 2)
        return pltpu.make_async_remote_copy(
            sendu.at[d, e], recvu.at[d, slot], early_send.at[d, e], early_recv.at[d, slot],
            device_id=(ring_to[d] - core + e, sec), device_id_type=MESH)

    def early_wait(d, slot):
        pltpu.make_async_remote_copy(
            sendu.at[d, slot], recvu.at[d, slot], early_send.at[d, slot], early_recv.at[d, slot],
            device_id=(ring_to[d], sec), device_id_type=MESH).wait_recv()

    pl.semaphore_wait(barrier, n_sec + 4)
    for e in range(2):
        for d in range(2):
            early_copy(d, e).start()

    len_swap = pltpu.make_async_remote_copy(
        lens.at[0], lens.at[1], len_sem.at[0], len_sem.at[1], device_id=(partner, sec), device_id_type=MESH)
    len_swap.start()

    xb_swap(owner(0)).start()
    for d in range(2):
        g_swap(d * PIECES + 1).start()

    def gram(acc, block, first):
        nt = (((1,), (1,)), ((), ()))
        left = lax.dot_general(block[:half], block[:half], nt, preferred_element_type=F32)
        right = lax.dot_general(block, block[half:], nt, preferred_element_type=F32)
        if first:
            acc[:half, :half] = left
            acc[:, half:] = right
        else:
            acc[:half, :half] += left
            acc[:, half:] += right

    x_copy.wait()
    span = 1024
    for j in range(xv.shape[1] // span):
        gram(gin, xv[:, j * span:(j + 1) * span], j == 0)

    @pl.loop(1, 3)
    def _(k):
        xb_swap(owner(k)).start()

    for s in list(range(2, PIECES)) + [0]:
        for d in range(2):
            g_swap(d * PIECES + s).start()

    @pl.loop(3, n_chips)
    def _(k):
        xb_swap(owner(k)).start()

    gram(gout, gv[0, :seq], True)
    gram(gout, gv[PIECES, :seq], False)

    @pl.loop(1, PIECES)
    def _(s):
        for d in range(2):
            c = d * PIECES + s
            g_copy(c).wait()
            gram(gout, gv[c, :seq], False)

    row = lax.broadcasted_iota(jnp.int32, (seq, half), 0)
    col = lax.broadcasted_iota(jnp.int32, (seq, half), 1)
    n_live = len_ref[0]
    left_live = (row[:half] < n_live) & (col[:half] < n_live)
    left = jnp.where(left_live, gin[:half, :half] * gout[:half, :half], 0.0)
    twice = jnp.where(row < half, 2.0, 1.0)
    right_live = (row < n_live) & (col + half < n_live)
    right = jnp.where(right_live, gin[:, half:] * gout[:, half:] * twice, 0.0)
    cells = left + right[:half] + right[half:]
    norm = jnp.sum(jnp.sum(cells, axis=0, keepdims=True), axis=1, keepdims=True)
    tile[...] = jnp.broadcast_to(norm, tile.shape)
    norms[sec] = tile[...]

    def norm_copy(j, frm, to):
        return pltpu.make_async_remote_copy(
            tile, norms.at[frm], norm_send.at[j], norm_recv.at[frm], device_id=(dp, to), device_id_type=MESH)

    @pl.loop(1, n_sec)
    def _(j):
        norm_copy(j, sec, lax.rem(sec + j, n_sec)).start()

    len_swap.wait_recv()
    token = lax.broadcasted_iota(jnp.int32, (seq, rows), 0).astype(F32)

    def turn(k):
        xb_copy(k).wait()
        xb_swap(k).wait_recv()
        for e in range(2):
            block = jnp.where(token < lens[e, 0:1, :], xb[e, k].astype(F32), 0.0)
            xt[k, :, e * seq:(e + 1) * seq] = block.T.astype(BF16)

    def scale(k):
        for e in range(2):
            factor = facs[e, 0:1, :]
            for j in range(seq // 128):
                cols = slice(e * seq + j * 128, e * seq + (j + 1) * 128)
                xt[k, :, cols] = (xt[k, :, cols].astype(F32) * factor).astype(BF16)

    turn(owner(0))
    for d in range(2):
        c = d * PIECES + 1
        g_swap(c).wait_recv()
        for e in range(2):
            tokens = slice(e * seq, (e + 1) * seq)
            pre[d, e] = jnp.dot(xt[owner(0), :, tokens], gv[c, tokens], preferred_element_type=F32)

    @pl.loop(1, 3)
    def _(k):
        turn(owner(k))

    @pl.loop(1, n_sec)
    def _(j):
        frm = lax.rem(sec + j, n_sec)
        norm_copy(j, frm, frm).wait_recv()

    total = jnp.sum(norms[...], axis=0)
    facs[0] = jnp.minimum(1.0, 1.0 / jnp.sqrt(total + 1e-06))
    fac_swap = pltpu.make_async_remote_copy(
        facs.at[0], facs.at[1], fac_sem.at[0], fac_sem.at[1], device_id=(partner, sec), device_id_type=MESH)
    fac_swap.start()
    fac_swap.wait_recv()

    def up_copy(d):
        return pltpu.make_async_remote_copy(
            facs, upfac.at[d], up_send.at[d], up_recv.at[d], device_id=(ring_to[d], sec), device_id_type=MESH)

    def ring_copy(d, i, s):
        return pltpu.make_async_remote_copy(
            sendb.at[d, i, s], recvb.at[d, i, s], ring_send.at[d, i, s], ring_recv.at[d, i, s],
            device_id=(ring_to[d], sec), device_id_type=MESH)

    def term(k, c):
        return jnp.dot(xt[k], gv[c], preferred_element_type=F32)

    def target(d, i):
        dist = n_chips // 2 - lax.div(i + 1, 2)
        return lax.rem(z + dist, n_chips) if d == 0 else lax.rem(z + n_chips - dist, n_chips)

    def chunk(d, i, s):
        return lax.rem(i + d, 2) * PIECES + s

    def place(n):
        return lax.div(n, PIECES), lax.rem(n, PIECES)

    def pieces(first, last, paced=True):
        @pl.loop(first, last)
        def _(n):
            i, s = place(n)
            for d in range(2):
                c = chunk(d, i, s)
                if last <= PIECES:
                    g_swap(c).wait_recv()
                part = term(target(d, i), c)
                if first == 2 * PIECES:
                    up_copy(d).wait_recv()
                    for e in range(2):
                        early_wait(d, e)
                        part += recvu[d, e].astype(F32) * across(upfac[d, e, 0:1])
                elif first > 2 * PIECES:
                    ring_copy(d, i - 2, s).wait_recv()
                    part += recvb[d, i - 2, s].astype(F32)
                sendb[d, i, s] = part.astype(BF16)
                if paced:
                    ring_copy(d, *place(n - 2)).wait_send()
                ring_copy(d, i, s).start()

    def across(factor):
        return jnp.concatenate([factor] * (width // 128), axis=1)

    for d in range(2):
        sendb[d, 0, 1] = (pre[d, 0] * across(facs[0, 0:1]) + pre[d, 1] * across(facs[1, 0:1])).astype(BF16)
        ring_copy(d, 0, 1).start()
    for d in range(2):
        up_copy(d).start()
    scale(owner(0))
    pieces(2, PIECES, paced=False)

    @pl.loop(1, 3)
    def _(k):
        scale(owner(k))

    for d in range(2):
        g_swap(d * PIECES).wait_recv()
    pieces(PIECES, 2 * PIECES)

    @pl.loop(3, n_chips)
    def _(k):
        turn(owner(k))
        scale(owner(k))

    pieces(2 * PIECES, 2 * PIECES + 1)
    pieces(2 * PIECES + 1, steps * PIECES)

    @pl.loop(0, PIECES)
    def _(s):
        for d in range(2):
            c = d * PIECES + s
            part = term(z, c)
            ring_copy(1 - d, steps - 2, s).wait_recv()
            fin[c] = part + recvb[1 - d, steps - 2, s].astype(F32)

    for s in range(PIECES):
        for d in range(2):
            c = d * PIECES + s
            ring_copy(d, steps - 1, s).wait_recv()
            done = (fin[c] + recvb[d, steps - 1, s].astype(F32)) * weight
            out_ref[:, c * width:(c + 1) * width] = done.astype(out_ref.dtype)

    len_swap.wait_send()
    fac_swap.wait_send()
    for d in range(2):
        up_copy(d).wait_send()
        for e in range(2):
            early_copy(d, e).wait_send()

    @pl.loop(1, n_sec)
    def _(j):
        norm_copy(j, sec, lax.rem(sec + j, n_sec)).wait_send()

    @pl.loop(0, chunks)
    def _(c):
        g_swap(c).wait_send()

    @pl.loop(0, n_chips)
    def _(k):
        xb_swap(k).wait_send()

    for d in range(2):
        for s in (PIECES - 2, PIECES - 1):
            ring_copy(d, steps - 1, s).wait_send()


def shards(layer_inputs, output_grads, lengths):
    n_dp, n_sec = lax.axis_size("dp"), lax.axis_size("section")
    inputs = layer_inputs[0, 0]
    grads = output_grads[0, 0]
    seq, din = inputs.shape
    dout = grads.shape[1]
    rows = din // n_dp
    n_chips = n_dp // 2
    chunks = 2 * PIECES
    width = dout // chunks
    weight = math.sqrt(din * dout * n_sec / n_dp)
    dma = pltpu.SemaphoreType.DMA
    ring = (2, n_chips - 1, PIECES)
    out = pl.pallas_call(
        functools.partial(kernel, (n_chips, n_sec, rows), weight),
        out_shape=jax.ShapeDtypeStruct((rows, dout), BF16),
        in_specs=[
            pl.BlockSpec(memory_space=pltpu.SMEM),
            pl.BlockSpec(memory_space=pl.ANY),
            pl.BlockSpec(memory_space=pl.ANY),
        ],
        out_specs=pl.BlockSpec(memory_space=pltpu.VMEM),
        scratch_shapes=[
            pltpu.VMEM((seq, din), BF16),
            pltpu.VMEM((2, n_chips, seq, rows), BF16),
            pltpu.VMEM((chunks, 2 * seq, width), BF16),
            pltpu.VMEM((n_chips, rows, 2 * seq), BF16),
            pltpu.VMEM(ring + (rows, width), BF16),
            pltpu.VMEM(ring + (rows, width), BF16),
            pltpu.VMEM((chunks, rows, width), F32),
            pltpu.VMEM((seq, seq), F32),
            pltpu.VMEM((seq, seq), F32),
            pltpu.VMEM((8, 128), F32),
            pltpu.VMEM((n_sec, 8, 128), F32),
            pltpu.VMEM((2, 8, 128), F32),
            pltpu.VMEM((2, 8, 128), F32),
            pltpu.VMEM((seq, 2 * rows), BF16),
            pltpu.VMEM((2, 2, rows, width), BF16),
            pltpu.VMEM((2, 2, rows, width), BF16),
            pltpu.VMEM((2, 2, 8, 128), F32),
            pltpu.VMEM((2, 2, rows, width), F32),
            dma,
            dma((2, 2)),
            dma((2, 2)),
            dma((2,)),
            dma((2,)),
            dma,
            dma((2, n_chips)),
            dma((2, chunks)),
            dma((n_chips,)),
            dma((chunks,)),
            dma((2,)),
            dma((n_sec,)),
            dma((n_sec,)),
            dma((2,)),
            dma(ring),
            dma(ring),
        ],
        compiler_params=pltpu.CompilerParams(
            collective_id=0, has_side_effects=True, vmem_limit_bytes=52 * 2**20
        ),
        cost_estimate=pl.CostEstimate(
            flops=2 * seq * din * dout + 2 * seq * seq * (din + dout), bytes_accessed=2 * seq * (din + dout),
            transcendentals=0,
        ),
    )(lengths, inputs, grads)
    return out[None]


def solution(mesh):
    placed = (P("section", "dp", None, None), P("section", "dp", None, None), P("dp"))
    return jax.shard_map(
        shards, mesh=mesh, in_specs=placed, out_specs=P("section", "dp", None), check_vma=False
    )
```

time: 221 us -> 112 us (0.51)
  waiting for transfers between devices: 115 us -> 0 us
  Pallas kernels: 0 us -> 110 us
  blocking collectives: 34.9 us -> 0 us
  local copies, waits for them, and re-layouts: 28.7 us -> 1.02 us
  matrix products: 24.4 us -> 0 us
  between operations: 14.9 us -> 0.66 us
    unnamed x2 -> x0, waiting for transfers between devices: 115 us -> none
    pallas_call x0 -> x1, Pallas kernels: none -> 110 us  [shards(): pl.pallas_call(functools.partial(kernel, (n_chips, n_sec, rows), weight),...]
    psum x1 -> x0, blocking collectives: 34.9 us -> none  [shards(): total = lax.psum(partial_norms, 'section')]
    unnamed x4 -> x1, local copies, waits for them, and re-layouts: 26.4 us -> 1.02 us
    dot_general x3 -> x0, matrix products: 24.4 us -> none  [the longest x1 15.9 us: shards(): lax.dot_general(flat_in, flat_out, (((0,), (0,)), ((), ())), preferred_el...]
    broadcast_in_dim x1 -> x0, local copies, waits for them, and re-layouts: 2.37 us -> none  [shards(): return (summed * weight).astype(jnp.bfloat16)[None]]
  transfers between devices with their start and end apart: 1 -> 0, of which waited for: 1 -> 0; matrix products, arithmetic and copies ran while one was open for 0% -> 0% of each run, Pallas kernels for 0% -> 0%
where the time goes in v1:
time: 112 us
  Pallas kernels  110 us (98%)
    pallas_call x1, Pallas kernels, shards(): pl.pallas_call(functools.partial(kernel, (n_chips, n_sec, rows), weight),...  110 us

profile of v1, /device:TPU:1, one launch (start us, length us, event | category | flops | bytes accessed | tf_op | source)
XLA Modules:
  0.0 111.5 jit_solution(589092061004759556)
XLA Ops:
  0.7 109.8 %shard_map.37 = bf16[128,4608]{1,0:T(8,128)(2,1)S(1)} custom-call(s32[1]{0:T(128)S(6)} %copy.5.len_ref, bf16[512,2048]{1,0:T(8,128)(2,1)} %bitcast.5, bf16[512,4608]{1,0:T(8,128)(2,1)} %bitcast.4), custom_call_target="tpu_custom_call" | custom-call | flops 13153337344 | bytes 6815744 | tf_op jit(solution)/shard_map/pallas_call | solution.py:344
  110.5 1.0 copy.6

commit v2 on v0

v2 whole, which is shorter than its diff:
```python
import functools
import math

import jax
import jax.numpy as jnp
from jax import lax
from jax.experimental import pallas as pl
from jax.experimental.pallas import tpu as pltpu
from jax.sharding import PartitionSpec as P

F32 = jnp.float32
BF16 = jnp.bfloat16
MESH = pl.DeviceIdType.MESH
PIECES = 3
EARLY = 2


def kernel(dims, weight, len_ref, x_ref, g_ref, out_ref, xe, xv, xb, gv, xt, sendb, recvb, sendu, recvu, pre, fin, gin, gout,
           row_tile, col_tile, rows_in, cols_in, lens, facs, upfac, xe_sem, xv_sem, g_sem, xb_send, xb_recv, g_send, g_recv,
           len_sem, row_send, row_recv, col_send, col_recv, early_send, early_recv, up_send, up_recv, ring_send, ring_recv):
    n_chips, side, rows = dims
    seq = x_ref.shape[0]
    half = sendb.shape[3]
    width = half // PIECES
    gone = EARLY * width
    mid = seq // 2
    steps = n_chips - 1
    dp = lax.axis_index("dp")
    sec = lax.axis_index("section")
    z = lax.div(dp, 2)
    core = lax.rem(dp, 2)
    partner = dp + 1 - 2 * core
    ahead = lax.rem(dp + 2, 2 * n_chips)
    behind = lax.rem(dp + 2 * n_chips - 2, 2 * n_chips)
    ring_to = (ahead, behind)
    sec_x = lax.div(sec, side)
    sec_y = lax.rem(sec, side)

    def in_row(j):
        return lax.rem(sec_x + j, side) * side + sec_y

    def in_col(j):
        return sec_x * side + lax.rem(sec_y + j, side)

    def owner(k):
        far = lax.div(k + 1, 2)
        turn = jnp.where(lax.rem(k, 2) == 1, n_chips - far, far)
        return lax.rem(z + n_chips // 2 + turn, n_chips)

    def x_cols(k, c):
        return pl.ds(pl.multiple_of((2 * k + c) * rows, 128), rows)

    def g_cols(h, part):
        return pl.ds(h * half + gone, half - gone) if part else pl.ds(h * half, gone)

    def g_copy(h, part):
        cols = g_cols(h, part)
        return pltpu.make_async_copy(g_ref.at[:, cols], gv.at[pl.ds(0, seq), cols], g_sem.at[h, part])

    def g_swap(h, part):
        cols = g_cols(h, part)
        return pltpu.make_async_remote_copy(
            g_ref.at[:, cols], gv.at[pl.ds(seq, seq), cols], g_send.at[h, part], g_recv.at[h, part],
            device_id=(partner, sec), device_id_type=MESH)

    def xb_swap(k):
        return pltpu.make_async_remote_copy(
            x_ref.at[:, x_cols(k, 1 - core)], xb.at[k], xb_send.at[k], xb_recv.at[k],
            device_id=(partner, sec), device_id_type=MESH)

    first = owner(0)
    xe_cols = pl.ds(pl.multiple_of(2 * first * rows, 128), 2 * rows)
    xe_copy = pltpu.make_async_copy(x_ref.at[:, xe_cols], xe, xe_sem)
    x_copy = pltpu.make_async_copy(x_ref, xv, xv_sem)
    xe_copy.start()
    for h in range(2):
        g_copy(h, 0).start()
    x_copy.start()
    for h in range(2):
        g_copy(h, 1).start()

    barrier = pltpu.get_barrier_semaphore()
    peers = [(peer + other, sec) for peer in ring_to for other in (0, partner - dp)]
    peers += [(dp, in_row(j)) for j in range(1, side)] + [(dp, in_col(j)) for j in range(1, side)]
    peers += [(partner, in_col(j)) for j in range(side)]
    for peer in peers:
        pl.semaphore_signal(barrier, inc=1, device_id=peer, device_id_type=MESH)

    xe_copy.wait()
    token = lax.broadcasted_iota(jnp.int32, xe.shape, 0)
    xet = jnp.where(token < len_ref[0], xe[...].astype(F32), 0.0).T.astype(BF16)

    def early_copy(d, p, e):
        slot = lax.rem(core + e, 2)
        return pltpu.make_async_remote_copy(
            sendu.at[d, p, e], recvu.at[d, p, slot], early_send.at[d, p, e], early_recv.at[d, p, slot],
            device_id=(ring_to[d] - core + e, sec), device_id_type=MESH)

    def early_wait(d, p, slot):
        pltpu.make_async_remote_copy(
            sendu.at[d, p, slot], recvu.at[d, p, slot], early_send.at[d, p, slot], early_recv.at[d, p, slot],
            device_id=(ring_to[d], sec), device_id_type=MESH).wait_recv()

    def early_terms(p):
        for d in range(2):
            if p == 0:
                g_copy(d, 0).wait()
            lo = d * half + p * width
            early = jnp.dot(xet, gv[:seq, lo:lo + width], preferred_element_type=F32).astype(BF16)
            for e in range(2):
                sendu[d, p, e] = early[e * rows:(e + 1) * rows]

    def early_start(p):
        for e in range(2):
            for d in range(2):
                early_copy(d, p, e).start()

    early_terms(0)
    lens[0] = jnp.full(lens.shape[1:], len_ref[0], F32)
    pl.semaphore_wait(barrier, len(peers))
    early_start(0)
    len_swap = pltpu.make_async_remote_copy(
        lens.at[0], lens.at[1], len_sem.at[0], len_sem.at[1], device_id=(partner, sec), device_id_type=MESH)
    len_swap.start()
    xb_swap(first).start()
    for h in range(2):
        g_swap(h, 1).start()

    def gram(acc, block, new=False):
        nt = (((1,), (1,)), ((), ()))
        left = lax.dot_general(block[:mid], block[:mid], nt, preferred_element_type=F32)
        right = lax.dot_general(block, block[mid:], nt, preferred_element_type=F32)
        if new:
            acc[:mid, :mid] = left
            acc[:, mid:] = right
        else:
            acc[:mid, :mid] += left
            acc[:, mid:] += right

    x_copy.wait()
    span = 1024
    for j in range(0, xv.shape[1], span):
        gram(gin, xv[:, j:j + span], j == 0)
    for p in range(1, EARLY):
        early_terms(p)
        early_start(p)
    for h in range(2):
        for j in range(0, gone, width):
            gram(gout, gv[:seq, h * half + j:h * half + j + width], h == 0 and j == 0)
    for h in range(2):
        g_copy(h, 1).wait()
        for j in range(gone, half, span):
            gram(gout, gv[:seq, h * half + j:h * half + min(j + span, half)])

    row = lax.broadcasted_iota(jnp.int32, (seq, mid), 0)
    col = lax.broadcasted_iota(jnp.int32, (seq, mid), 1)
    n_live = len_ref[0]
    left_live = (row[:mid] < n_live) & (col[:mid] < n_live)
    left = jnp.where(left_live, gin[:mid, :mid] * gout[:mid, :mid], 0.0)
    twice = jnp.where(row < mid, 2.0, 1.0)
    right_live = (row < n_live) & (col + mid < n_live)
    right = jnp.where(right_live, gin[:, mid:] * gout[:, mid:] * twice, 0.0)
    cells = left + right[:mid] + right[mid:]
    norm = jnp.sum(jnp.sum(cells, axis=0, keepdims=True), axis=1, keepdims=True)
    row_tile[...] = jnp.broadcast_to(norm, row_tile.shape)

    def row_copy(j, frm):
        return pltpu.make_async_remote_copy(
            row_tile, rows_in.at[frm], row_send.at[j], row_recv.at[frm], device_id=(dp, in_row(j)), device_id_type=MESH)

    def col_copy(e, j, frm):
        return pltpu.make_async_remote_copy(
            col_tile, cols_in.at[e, frm], col_send.at[e, j], col_recv.at[e, frm],
            device_id=(partner if e else dp, in_col(j)), device_id_type=MESH)

    for j in range(1, side):
        row_copy(j, sec_x).start()
    rows_in[sec_x] = row_tile[...]

    token = lax.broadcasted_iota(jnp.int32, (seq, rows), 0).astype(F32)

    def turn(k):
        xb_swap(k).wait_recv()
        for e, block in enumerate((xv[:, x_cols(k, core)], xb[k])):
            block = jnp.where(token < lens[e, 0:1, :], block.astype(F32), 0.0)
            xt[k, :, e * seq:(e + 1) * seq] = block.T.astype(BF16)

    def scale(k):
        for e in range(2):
            factor = facs[e, 0:1, :]
            for j in range(seq // 128):
                cols = slice(e * seq + j * 128, e * seq + (j + 1) * 128)
                xt[k, :, cols] = (xt[k, :, cols].astype(F32) * factor).astype(BF16)

    len_swap.wait_recv()
    turn(first)

    for j in range(1, side):
        row_copy(j, lax.rem(sec_x + j, side)).wait_recv()
    col_tile[...] = jnp.sum(rows_in[...], axis=0)
    for j in range(side):
        col_copy(1, j, sec_y).start()
        if j:
            col_copy(0, j, sec_y).start()
    cols_in[0, sec_y] = col_tile[...]

    rest = [(s * width, (s + 1) * width) for s in range(EARLY, PIECES)]
    for d in range(2):
        g_swap(d, 1).wait_recv()
        for lo, hi in rest:
            for e in range(2):
                tokens = slice(e * seq, (e + 1) * seq)
                pre[d, e, :, lo - gone:hi - gone] = jnp.dot(
                    xt[first, :, tokens], gv[tokens, d * half + lo:d * half + hi], preferred_element_type=F32)

    for j in range(side):
        frm = lax.rem(sec_y + j, side)
        col_copy(1, j, frm).wait_recv()
        if j:
            col_copy(0, j, frm).wait_recv()
    for e in range(2):
        facs[e] = jnp.minimum(1.0, 1.0 / jnp.sqrt(jnp.sum(cols_in[e], axis=0) + 1e-06))

    def up_copy(d):
        return pltpu.make_async_remote_copy(
            facs, upfac.at[d], up_send.at[d], up_recv.at[d], device_id=(ring_to[d], sec), device_id_type=MESH)

    def ring_copy(d, i, part=0):
        block = pl.ds(0, half)
        if isinstance(i, int) and i == 0:
            block = pl.ds(gone, half - gone)
        elif isinstance(i, int) and i == steps - 1:
            block = pl.ds(half - width, width) if part else pl.ds(0, half - width)
        return pltpu.make_async_remote_copy(
            sendb.at[d, i, :, block], recvb.at[d, i, :, block], ring_send.at[d, i + part], ring_recv.at[d, i + part],
            device_id=(ring_to[d], sec), device_id_type=MESH)

    def term(k, h, s):
        return jnp.dot(xt[k], gv[:, pl.ds(pl.multiple_of(h * half + s * width, 128), width)], preferred_element_type=F32)

    def target(d, i):
        dist = n_chips // 2 - lax.div(i + 1, 2)
        return lax.rem(z + dist, n_chips) if d == 0 else lax.rem(z + n_chips - dist, n_chips)

    def cols(s):
        return slice(s * width, (s + 1) * width)

    def across(factor, n):
        return jnp.concatenate([factor] * (n // 128), axis=1)

    def step(i, add=True):
        for d in range(2):
            for s in range(PIECES):
                part = term(target(d, i), lax.rem(i + d, 2), s)
                if add:
                    if s == 0:
                        ring_copy(d, i - 2).wait_recv()
                    part += recvb[d, i - 2, :, cols(s)].astype(F32)
                sendb[d, i, :, cols(s)] = part.astype(BF16)
                if isinstance(i, int) and i == steps - 1 and s == PIECES - 2:
                    ring_copy(d, i).start()
            ring_copy(d, i, isinstance(i, int) and i == steps - 1).start()

    for d in range(2):
        for lo, hi in rest:
            own, other = (pre[d, e, :, lo - gone:hi - gone] * across(facs[e, 0:1], hi - lo) for e in range(2))
            sendb[d, 0, :, lo:hi] = (own + other).astype(BF16)
        ring_copy(d, 0).start()
    for k in (1, 2):
        xb_swap(owner(k)).start()
    for h in range(2):
        g_swap(h, 0).start()
    for d in range(2):
        up_copy(d).start()

    @pl.loop(3, n_chips)
    def _(k):
        xb_swap(owner(k)).start()

    @pl.loop(1, 3)
    def _(k):
        turn(owner(k))
        scale(owner(k))

    for h in range(2):
        g_swap(h, 0).wait_recv()
    step(1, add=False)

    @pl.loop(3, n_chips)
    def _(k):
        turn(owner(k))
        scale(owner(k))

    for d in range(2):
        for s in range(PIECES):
            part = term(target(d, 2), d, s)
            if s == 0:
                up_copy(d).wait_recv()
            if s < EARLY:
                for e in range(2):
                    early_wait(d, s, e)
                    part += recvu[d, s, e].astype(F32) * across(upfac[d, e, 0:1], width)
            else:
                if s == EARLY:
                    ring_copy(d, 0).wait_recv()
                part += recvb[d, 0, :, cols(s)].astype(F32)
            sendb[d, 2, :, cols(s)] = part.astype(BF16)
        ring_copy(d, 2).start()

    @pl.loop(3, steps - 1)
    def _(i):
        step(i)

    step(steps - 1)

    for d in range(2):
        for s in range(PIECES):
            part = term(z, d, s)
            if s == 0:
                ring_copy(1 - d, steps - 2).wait_recv()
            fin[d * PIECES + s] = part + recvb[1 - d, steps - 2, :, cols(s)].astype(F32)

    for s in range(PIECES):
        for d in range(2):
            c = d * PIECES + s
            if s == 0 or s == PIECES - 1:
                ring_copy(d, steps - 1, int(s > 0)).wait_recv()
            done = (fin[c] + recvb[d, steps - 1, :, cols(s)].astype(F32)) * weight
            out_ref[:, cols(c)] = done.astype(out_ref.dtype)

    len_swap.wait_send()
    for d in range(2):
        up_copy(d).wait_send()
        for e in range(2):
            for p in range(EARLY):
                early_copy(d, p, e).wait_send()
            g_swap(d, e).wait_send()
        for i in range(steps):
            ring_copy(d, i).wait_send()
        ring_copy(d, steps - 1, 1).wait_send()
    for j in range(side):
        col_copy(1, j, sec_y).wait_send()
        if j:
            row_copy(j, sec_x).wait_send()
            col_copy(0, j, sec_y).wait_send()

    @pl.loop(0, n_chips)
    def _(k):
        xb_swap(k).wait_send()


def shards(layer_inputs, output_grads, lengths):
    n_dp, n_sec = lax.axis_size("dp"), lax.axis_size("section")
    inputs = layer_inputs[0, 0]
    grads = output_grads[0, 0]
    seq, din = inputs.shape
    dout = grads.shape[1]
    rows = din // n_dp
    n_chips = n_dp // 2
    steps = n_chips - 1
    half = dout // 2
    width = half // PIECES
    side = math.isqrt(n_sec)
    weight = math.sqrt(din * dout * n_sec / n_dp)
    dma = pltpu.SemaphoreType.DMA
    vmem = pltpu.VMEM
    out = pl.pallas_call(
        functools.partial(kernel, (n_chips, side, rows), weight),
        out_shape=jax.ShapeDtypeStruct((rows, dout), BF16),
        in_specs=[
            pl.BlockSpec(memory_space=pltpu.SMEM),
            pl.BlockSpec(memory_space=pl.ANY),
            pl.BlockSpec(memory_space=pl.ANY),
        ],
        out_specs=pl.BlockSpec(memory_space=pltpu.VMEM),
        scratch_shapes=dict(
            xe=vmem((seq, 2 * rows), BF16),
            xv=vmem((seq, din), BF16),
            xb=vmem((n_chips, seq, rows), BF16),
            gv=vmem((2 * seq, dout), BF16),
            xt=vmem((n_chips, rows, 2 * seq), BF16),
            sendb=vmem((2, steps, rows, half), BF16),
            recvb=vmem((2, steps, rows, half), BF16),
            sendu=vmem((2, EARLY, 2, rows, width), BF16),
            recvu=vmem((2, EARLY, 2, rows, width), BF16),
            pre=vmem((2, 2, rows, (PIECES - EARLY) * width), F32),
            fin=vmem((2 * PIECES, rows, width), F32),
            gin=vmem((seq, seq), F32),
            gout=vmem((seq, seq), F32),
            row_tile=vmem((8, 128), F32),
            col_tile=vmem((8, 128), F32),
            rows_in=vmem((side, 8, 128), F32),
            cols_in=vmem((2, side, 8, 128), F32),
            lens=vmem((2, 8, 128), F32),
            facs=vmem((2, 8, 128), F32),
            upfac=vmem((2, 2, 8, 128), F32),
            xe_sem=dma,
            xv_sem=dma,
            g_sem=dma((2, 2)),
            xb_send=dma((n_chips,)),
            xb_recv=dma((n_chips,)),
            g_send=dma((2, 2)),
            g_recv=dma((2, 2)),
            len_sem=dma((2,)),
            row_send=dma((side,)),
            row_recv=dma((side,)),
            col_send=dma((2, side)),
            col_recv=dma((2, side)),
            early_send=dma((2, EARLY, 2)),
            early_recv=dma((2, EARLY, 2)),
            up_send=dma((2,)),
            up_recv=dma((2,)),
            ring_send=dma((2, steps + 1)),
            ring_recv=dma((2, steps + 1)),
        ),
        compiler_params=pltpu.CompilerParams(
            collective_id=0, has_side_effects=True, vmem_limit_bytes=52 * 2**20
        ),
        cost_estimate=pl.CostEstimate(
            flops=2 * seq * din * dout + 2 * seq * seq * (din + dout), bytes_accessed=2 * seq * (din + dout),
            transcendentals=0,
        ),
    )(lengths, inputs, grads)
    return out[None]


def solution(mesh):
    placed = (P("section", "dp", None, None), P("section", "dp", None, None), P("dp"))
    return jax.shard_map(
        shards, mesh=mesh, in_specs=placed, out_specs=P("section", "dp", None), check_vma=False
    )
```

time: 221 us -> 111 us (0.50)
  waiting for transfers between devices: 115 us -> 0 us
  Pallas kernels: 0 us -> 110 us
  blocking collectives: 34.9 us -> 0 us
  local copies, waits for them, and re-layouts: 28.7 us -> 1.02 us
  matrix products: 24.4 us -> 0 us
  between operations: 14.9 us -> 0.66 us
    unnamed x2 -> x0, waiting for transfers between devices: 115 us -> none
    pallas_call x0 -> x1, Pallas kernels: none -> 110 us  [shards(): pl.pallas_call(functools.partial(kernel, (n_chips, side, rows), weight),...]
    psum x1 -> x0, blocking collectives: 34.9 us -> none  [shards(): total = lax.psum(partial_norms, 'section')]
    unnamed x4 -> x1, local copies, waits for them, and re-layouts: 26.4 us -> 1.02 us
    dot_general x3 -> x0, matrix products: 24.4 us -> none  [the longest x1 15.9 us: shards(): lax.dot_general(flat_in, flat_out, (((0,), (0,)), ((), ())), preferred_el...]
    broadcast_in_dim x1 -> x0, local copies, waits for them, and re-layouts: 2.37 us -> none  [shards(): return (summed * weight).astype(jnp.bfloat16)[None]]
  transfers between devices with their start and end apart: 1 -> 0, of which waited for: 1 -> 0; matrix products, arithmetic and copies ran while one was open for 0% -> 0% of each run, Pallas kernels for 0% -> 0%
where the time goes in v2:
time: 111 us
  Pallas kernels  110 us (99%)
    pallas_call x1, Pallas kernels, shards(): pl.pallas_call(functools.partial(kernel, (n_chips, side, rows), weight),...  110 us

profile of v2, /device:TPU:1, one launch (start us, length us, event | category | flops | bytes accessed | tf_op | source)
XLA Modules:
  0.0 111.2 jit_solution(10070748381483867096)
XLA Ops:
  0.7 109.5 %shard_map.37 = bf16[128,4608]{1,0:T(8,128)(2,1)S(1)} custom-call(s32[1]{0:T(128)S(6)} %copy.5.len_ref, bf16[512,2048]{1,0:T(8,128)(2,1)} %bitcast.5, bf16[512,4608]{1,0:T(8,128)(2,1)} %bitcast.4), custom_call_target="tpu_custom_call" | custom-call | flops 13153337344 | bytes 6815744 | tf_op jit(solution)/shard_map/pallas_call | solution.py:367
  110.2 1.0 copy.6

commit v3 on v2

--- a/solution.py
+++ b/solution.py
@@ -13,6 +13,7 @@
 MESH = pl.DeviceIdType.MESH
 PIECES = 3
 EARLY = 2
+PART = 512
 
 
 def kernel(dims, weight, len_ref, x_ref, g_ref, out_ref, xe, xv, xb, gv, xt, sendb, recvb, sendu, recvu, pre, fin, gin, gout,
@@ -22,7 +23,7 @@
     seq = x_ref.shape[0]
     half = sendb.shape[3]
     width = half // PIECES
-    gone = EARLY * width
+    gone = EARLY * PART
     mid = seq // 2
     steps = n_chips - 1
     dp = lax.axis_index("dp")
@@ -105,8 +106,8 @@
         for d in range(2):
             if p == 0:
                 g_copy(d, 0).wait()
-            lo = d * half + p * width
-            early = jnp.dot(xet, gv[:seq, lo:lo + width], preferred_element_type=F32).astype(BF16)
+            lo = d * half + p * PART
+            early = jnp.dot(xet, gv[:seq, lo:lo + PART], preferred_element_type=F32).astype(BF16)
             for e in range(2):
                 sendu[d, p, e] = early[e * rows:(e + 1) * rows]
 
@@ -138,19 +139,13 @@
             acc[:, mid:] += right
 
     x_copy.wait()
-    span = 1024
-    for j in range(0, xv.shape[1], span):
-        gram(gin, xv[:, j:j + span], j == 0)
+    gram(gin, xv[...], True)
     for p in range(1, EARLY):
         early_terms(p)
         early_start(p)
     for h in range(2):
-        for j in range(0, gone, width):
-            gram(gout, gv[:seq, h * half + j:h * half + j + width], h == 0 and j == 0)
-    for h in range(2):
         g_copy(h, 1).wait()
-        for j in range(gone, half, span):
-            gram(gout, gv[:seq, h * half + j:h * half + min(j + span, half)])
+        gram(gout, gv[:seq, h * half:(h + 1) * half], h == 0)
 
     row = lax.broadcasted_iota(jnp.int32, (seq, mid), 0)
     col = lax.broadcasted_iota(jnp.int32, (seq, mid), 1)
@@ -192,9 +187,6 @@
                 cols = slice(e * seq + j * 128, e * seq + (j + 1) * 128)
                 xt[k, :, cols] = (xt[k, :, cols].astype(F32) * factor).astype(BF16)
 
-    len_swap.wait_recv()
-    turn(first)
-
     for j in range(1, side):
         row_copy(j, lax.rem(sec_x + j, side)).wait_recv()
     col_tile[...] = jnp.sum(rows_in[...], axis=0)
@@ -204,7 +196,9 @@
             col_copy(0, j, sec_y).start()
     cols_in[0, sec_y] = col_tile[...]
 
-    rest = [(s * width, (s + 1) * width) for s in range(EARLY, PIECES)]
+    len_swap.wait_recv()
+    turn(first)
+    rest = [(lo, min(lo + width, half)) for lo in range(gone, half, width)]
     for d in range(2):
         g_swap(d, 1).wait_recv()
         for lo, hi in rest:
@@ -292,19 +286,19 @@
         scale(owner(k))
 
     for d in range(2):
-        for s in range(PIECES):
-            part = term(target(d, 2), d, s)
-            if s == 0:
-                up_copy(d).wait_recv()
-            if s < EARLY:
-                for e in range(2):
-                    early_wait(d, s, e)
-                    part += recvu[d, s, e].astype(F32) * across(upfac[d, e, 0:1], width)
-            else:
-                if s == EARLY:
-                    ring_copy(d, 0).wait_recv()
-                part += recvb[d, 0, :, cols(s)].astype(F32)
-            sendb[d, 2, :, cols(s)] = part.astype(BF16)
+        up_copy(d).wait_recv()
+        for p in range(EARLY):
+            lo, hi = p * PART, (p + 1) * PART
+            part = jnp.dot(xt[target(d, 2)], gv[:, d * half + lo:d * half + hi], preferred_element_type=F32)
+            for e in range(2):
+                early_wait(d, p, e)
+                part += recvu[d, p, e].astype(F32) * across(upfac[d, e, 0:1], PART)
+            sendb[d, 2, :, lo:hi] = part.astype(BF16)
+        for lo, hi in rest:
+            part = jnp.dot(xt[target(d, 2)], gv[:, d * half + lo:d * half + hi], preferred_element_type=F32)
+            if lo == gone:
+                ring_copy(d, 0).wait_recv()
+            sendb[d, 2, :, lo:hi] = (part + recvb[d, 0, :, lo:hi].astype(F32)).astype(BF16)
         ring_copy(d, 2).start()
 
     @pl.loop(3, steps - 1)
@@ -381,9 +375,9 @@
             xt=vmem((n_chips, rows, 2 * seq), BF16),
             sendb=vmem((2, steps, rows, half), BF16),
             recvb=vmem((2, steps, rows, half), BF16),
-            sendu=vmem((2, EARLY, 2, rows, width), BF16),
-            recvu=vmem((2, EARLY, 2, rows, width), BF16),
-            pre=vmem((2, 2, rows, (PIECES - EARLY) * width), F32),
+            sendu=vmem((2, EARLY, 2, rows, PART), BF16),
+            recvu=vmem((2, EARLY, 2, rows, PART), BF16),
+            pre=vmem((2, 2, rows, half - EARLY * PART), F32),
             fin=vmem((2 * PIECES, rows, width), F32),
             gin=vmem((seq, seq), F32),
             gout=vmem((seq, seq), F32),

time: 111 us -> 109 us (0.982)
  Pallas kernels: 110 us -> 108 us
    pallas_call x1, Pallas kernels: 110 us -> 108 us  [shards(): pl.pallas_call(functools.partial(kernel, (n_chips, side, rows), weight),...]
where the time goes in v3:
time: 109 us
  Pallas kernels  108 us (99%)
    pallas_call x1, Pallas kernels, shards(): pl.pallas_call(functools.partial(kernel, (n_chips, side, rows), weight),...  108 us

profile of v3, /device:TPU:1, one launch (start us, length us, event | category | flops | bytes accessed | tf_op | source)
XLA Modules:
  0.0 109.4 jit_solution(4875322733329844076)
XLA Ops:
  0.7 107.7 %shard_map.37 = bf16[128,4608]{1,0:T(8,128)(2,1)S(1)} custom-call(s32[1]{0:T(128)S(6)} %copy.5.len_ref, bf16[512,2048]{1,0:T(8,128)(2,1)} %bitcast.5, bf16[512,4608]{1,0:T(8,128)(2,1)} %bitcast.4), custom_call_target="tpu_custom_call" | custom-call | flops 13153337344 | bytes 6815744 | tf_op jit(solution)/shard_map/pallas_call | solution.py:361
  108.4 1.0 copy.6

commit v4 on v3

--- a/solution.py
+++ b/solution.py
@@ -12,8 +12,7 @@
 BF16 = jnp.bfloat16
 MESH = pl.DeviceIdType.MESH
 PIECES = 3
-EARLY = 2
-PART = 512
+EARLY = ((0, 512), (512, 896))
 
 
 def kernel(dims, weight, len_ref, x_ref, g_ref, out_ref, xe, xv, xb, gv, xt, sendb, recvb, sendu, recvu, pre, fin, gin, gout,
@@ -23,7 +22,8 @@
     seq = x_ref.shape[0]
     half = sendb.shape[3]
     width = half // PIECES
-    gone = EARLY * PART
+    gone = EARLY[-1][1]
+    rest = ((gone, half - width), (half - width, half))
     mid = seq // 2
     steps = n_chips - 1
     dp = lax.axis_index("dp")
@@ -76,9 +76,6 @@
     xe_copy.start()
     for h in range(2):
         g_copy(h, 0).start()
-    x_copy.start()
-    for h in range(2):
-        g_copy(h, 1).start()
 
     barrier = pltpu.get_barrier_semaphore()
     peers = [(peer + other, sec) for peer in ring_to for other in (0, partner - dp)]
@@ -86,35 +83,33 @@
     peers += [(partner, in_col(j)) for j in range(side)]
     for peer in peers:
         pl.semaphore_signal(barrier, inc=1, device_id=peer, device_id_type=MESH)
+    x_copy.start()
+    for h in range(2):
+        g_copy(h, 1).start()
 
     xe_copy.wait()
     token = lax.broadcasted_iota(jnp.int32, xe.shape, 0)
     xet = jnp.where(token < len_ref[0], xe[...].astype(F32), 0.0).T.astype(BF16)
 
-    def early_copy(d, p, e):
-        slot = lax.rem(core + e, 2)
-        return pltpu.make_async_remote_copy(
-            sendu.at[d, p, e], recvu.at[d, p, slot], early_send.at[d, p, e], early_recv.at[d, p, slot],
+    def early_copy(d, p, e, slot):
+        block = pl.ds(EARLY[p][0], EARLY[p][1] - EARLY[p][0])
+        return pltpu.make_async_remote_copy(
+            sendu.at[d, e, :, block], recvu.at[d, slot, :, block], early_send.at[d, p, e], early_recv.at[d, p, slot],
             device_id=(ring_to[d] - core + e, sec), device_id_type=MESH)
-
-    def early_wait(d, p, slot):
-        pltpu.make_async_remote_copy(
-            sendu.at[d, p, slot], recvu.at[d, p, slot], early_send.at[d, p, slot], early_recv.at[d, p, slot],
-            device_id=(ring_to[d], sec), device_id_type=MESH).wait_recv()
 
     def early_terms(p):
         for d in range(2):
             if p == 0:
                 g_copy(d, 0).wait()
-            lo = d * half + p * PART
-            early = jnp.dot(xet, gv[:seq, lo:lo + PART], preferred_element_type=F32).astype(BF16)
+            lo, hi = EARLY[p]
+            early = jnp.dot(xet, gv[:seq, d * half + lo:d * half + hi], preferred_element_type=F32).astype(BF16)
             for e in range(2):
-                sendu[d, p, e] = early[e * rows:(e + 1) * rows]
+                sendu[d, e, :, lo:hi] = early[e * rows:(e + 1) * rows]
 
     def early_start(p):
         for e in range(2):
             for d in range(2):
-                early_copy(d, p, e).start()
+                early_copy(d, p, e, lax.rem(core + e, 2)).start()
 
     early_terms(0)
     lens[0] = jnp.full(lens.shape[1:], len_ref[0], F32)
@@ -140,9 +135,6 @@
 
     x_copy.wait()
     gram(gin, xv[...], True)
-    for p in range(1, EARLY):
-        early_terms(p)
-        early_start(p)
     for h in range(2):
         g_copy(h, 1).wait()
         gram(gout, gv[:seq, h * half:(h + 1) * half], h == 0)
@@ -171,6 +163,9 @@
     for j in range(1, side):
         row_copy(j, sec_x).start()
     rows_in[sec_x] = row_tile[...]
+    for p in range(1, len(EARLY)):
+        early_terms(p)
+        early_start(p)
 
     token = lax.broadcasted_iota(jnp.int32, (seq, rows), 0).astype(F32)
 
@@ -198,14 +193,13 @@
 
     len_swap.wait_recv()
     turn(first)
-    rest = [(lo, min(lo + width, half)) for lo in range(gone, half, width)]
+    lo, hi = rest[0]
     for d in range(2):
         g_swap(d, 1).wait_recv()
-        for lo, hi in rest:
-            for e in range(2):
-                tokens = slice(e * seq, (e + 1) * seq)
-                pre[d, e, :, lo - gone:hi - gone] = jnp.dot(
-                    xt[first, :, tokens], gv[tokens, d * half + lo:d * half + hi], preferred_element_type=F32)
+        for e in range(2):
+            tokens = slice(e * seq, (e + 1) * seq)
+            pre[d, e] = jnp.dot(
+                xt[first, :, tokens], gv[tokens, d * half + lo:d * half + hi], preferred_element_type=F32)
 
     for j in range(side):
         frm = lax.rem(sec_y + j, side)
@@ -221,12 +215,14 @@
 
     def ring_copy(d, i, part=0):
         block = pl.ds(0, half)
+        sem = i + part
         if isinstance(i, int) and i == 0:
-            block = pl.ds(gone, half - gone)
+            block = pl.ds(rest[part][0], rest[part][1] - rest[part][0])
+            sem = part * (steps + 1)
         elif isinstance(i, int) and i == steps - 1:
             block = pl.ds(half - width, width) if part else pl.ds(0, half - width)
         return pltpu.make_async_remote_copy(
-            sendb.at[d, i, :, block], recvb.at[d, i, :, block], ring_send.at[d, i + part], ring_recv.at[d, i + part],
+            sendb.at[d, i, :, block], recvb.at[d, i, :, block], ring_send.at[d, sem], ring_recv.at[d, sem],
             device_id=(ring_to[d], sec), device_id_type=MESH)
 
     def term(k, h, s):
@@ -255,11 +251,17 @@
                     ring_copy(d, i).start()
             ring_copy(d, i, isinstance(i, int) and i == steps - 1).start()
 
-    for d in range(2):
-        for lo, hi in rest:
-            own, other = (pre[d, e, :, lo - gone:hi - gone] * across(facs[e, 0:1], hi - lo) for e in range(2))
-            sendb[d, 0, :, lo:hi] = (own + other).astype(BF16)
+    lo, hi = rest[0]
+    for d in range(2):
+        own, other = (pre[d, e] * across(facs[e, 0:1], hi - lo) for e in range(2))
+        sendb[d, 0, :, lo:hi] = (own + other).astype(BF16)
         ring_copy(d, 0).start()
+    scale(first)
+    lo, hi = rest[1]
+    for d in range(2):
+        part = jnp.dot(xt[first], gv[:, d * half + lo:d * half + hi], preferred_element_type=F32)
+        sendb[d, 0, :, lo:hi] = part.astype(BF16)
+        ring_copy(d, 0, 1).start()
     for k in (1, 2):
         xb_swap(owner(k)).start()
     for h in range(2):
@@ -287,17 +289,15 @@
 
     for d in range(2):
         up_copy(d).wait_recv()
-        for p in range(EARLY):
-            lo, hi = p * PART, (p + 1) * PART
+        for p, (lo, hi) in enumerate(EARLY):
             part = jnp.dot(xt[target(d, 2)], gv[:, d * half + lo:d * half + hi], preferred_element_type=F32)
             for e in range(2):
-                early_wait(d, p, e)
-                part += recvu[d, p, e].astype(F32) * across(upfac[d, e, 0:1], PART)
+                early_copy(d, p, e, e).wait_recv()
+                part += recvu[d, e, :, lo:hi].astype(F32) * across(upfac[d, e, 0:1], hi - lo)
             sendb[d, 2, :, lo:hi] = part.astype(BF16)
-        for lo, hi in rest:
+        for p, (lo, hi) in enumerate(rest):
             part = jnp.dot(xt[target(d, 2)], gv[:, d * half + lo:d * half + hi], preferred_element_type=F32)
-            if lo == gone:
-                ring_copy(d, 0).wait_recv()
+            ring_copy(d, 0, p).wait_recv()
             sendb[d, 2, :, lo:hi] = (part + recvb[d, 0, :, lo:hi].astype(F32)).astype(BF16)
         ring_copy(d, 2).start()
 
@@ -326,12 +326,13 @@
     for d in range(2):
         up_copy(d).wait_send()
         for e in range(2):
-            for p in range(EARLY):
-                early_copy(d, p, e).wait_send()
+            for p in range(len(EARLY)):
+                early_copy(d, p, e, e).wait_send()
             g_swap(d, e).wait_send()
         for i in range(steps):
             ring_copy(d, i).wait_send()
-        ring_copy(d, steps - 1, 1).wait_send()
+        for i in (0, steps - 1):
+            ring_copy(d, i, 1).wait_send()
     for j in range(side):
         col_copy(1, j, sec_y).wait_send()
         if j:
@@ -355,6 +356,7 @@
     half = dout // 2
     width = half // PIECES
     side = math.isqrt(n_sec)
+    gone = EARLY[-1][1]
     weight = math.sqrt(din * dout * n_sec / n_dp)
     dma = pltpu.SemaphoreType.DMA
     vmem = pltpu.VMEM
@@ -375,9 +377,9 @@
             xt=vmem((n_chips, rows, 2 * seq), BF16),
             sendb=vmem((2, steps, rows, half), BF16),
             recvb=vmem((2, steps, rows, half), BF16),
-            sendu=vmem((2, EARLY, 2, rows, PART), BF16),
-            recvu=vmem((2, EARLY, 2, rows, PART), BF16),
-            pre=vmem((2, 2, rows, half - EARLY * PART), F32),
+            sendu=vmem((2, 2, rows, gone), BF16),
+            recvu=vmem((2, 2, rows, gone), BF16),
+            pre=vmem((2, 2, rows, half - width - gone), F32),
             fin=vmem((2 * PIECES, rows, width), F32),
             gin=vmem((seq, seq), F32),
             gout=vmem((seq, seq), F32),
@@ -400,12 +402,12 @@
             row_recv=dma((side,)),
             col_send=dma((2, side)),
             col_recv=dma((2, side)),
-            early_send=dma((2, EARLY, 2)),
-            early_recv=dma((2, EARLY, 2)),
+            early_send=dma((2, len(EARLY), 2)),
+            early_recv=dma((2, len(EARLY), 2)),
             up_send=dma((2,)),
             up_recv=dma((2,)),
-            ring_send=dma((2, steps + 1)),
-            ring_recv=dma((2, steps + 1)),
+            ring_send=dma((2, steps + 2)),
+            ring_recv=dma((2, steps + 2)),
         ),
         compiler_params=pltpu.CompilerParams(
             collective_id=0, has_side_effects=True, vmem_limit_bytes=52 * 2**20

time: 109 us -> 111 us (1.018)
  no operation moved by 1% of the time
where the time goes in v4:
time: 111 us; the launch traced here: 110 us
  Pallas kernels  109 us (98%)
    pallas_call x1, Pallas kernels, shards(): pl.pallas_call(functools.partial(kernel, (n_chips, side, rows), weight),...  109 us

profile of v4, /device:TPU:1, one launch (start us, length us, event | category | flops | bytes accessed | tf_op | source)
XLA Modules:
  0.0 110.4 jit_solution(946541440739262682)
XLA Ops:
  0.7 108.8 %shard_map.37 = bf16[128,4608]{1,0:T(8,128)(2,1)S(1)} custom-call(s32[1]{0:T(128)S(6)} %copy.5.len_ref, bf16[512,2048]{1,0:T(8,128)(2,1)} %bitcast.5, bf16[512,4608]{1,0:T(8,128)(2,1)} %bitcast.4), custom_call_target="tpu_custom_call" | custom-call | flops 13153337344 | bytes 6815744 | tf_op jit(solution)/shard_map/pallas_call | solution.py:363
  109.4 1.0 copy.6

commit v5 on v3

--- a/solution.py
+++ b/solution.py
@@ -195,6 +195,10 @@
         if j:
             col_copy(0, j, sec_y).start()
     cols_in[0, sec_y] = col_tile[...]
+    for k in (1, 2):
+        xb_swap(owner(k)).start()
+    for h in range(2):
+        g_swap(h, 0).start()
 
     len_swap.wait_recv()
     turn(first)
@@ -260,10 +264,6 @@
             own, other = (pre[d, e, :, lo - gone:hi - gone] * across(facs[e, 0:1], hi - lo) for e in range(2))
             sendb[d, 0, :, lo:hi] = (own + other).astype(BF16)
         ring_copy(d, 0).start()
-    for k in (1, 2):
-        xb_swap(owner(k)).start()
-    for h in range(2):
-        g_swap(h, 0).start()
     for d in range(2):
         up_copy(d).start()
 

time: 109 us -> 109 us (level)
  no operation moved by 1% of the time
where the time goes in v5:
time: 109 us
  Pallas kernels  108 us (99%)
    pallas_call x1, Pallas kernels, shards(): pl.pallas_call(functools.partial(kernel, (n_chips, side, rows), weight),...  108 us

profile of v5, /device:TPU:1, one launch (start us, length us, event | category | flops | bytes accessed | tf_op | source)
XLA Modules:
  0.0 109.4 jit_solution(17081028089067253329)
XLA Ops:
  0.7 107.7 %shard_map.37 = bf16[128,4608]{1,0:T(8,128)(2,1)S(1)} custom-call(s32[1]{0:T(128)S(6)} %copy.5.len_ref, bf16[512,2048]{1,0:T(8,128)(2,1)} %bitcast.5, bf16[512,4608]{1,0:T(8,128)(2,1)} %bitcast.4), custom_call_target="tpu_custom_call" | custom-call | flops 13153337344 | bytes 6815744 | tf_op jit(solution)/shard_map/pallas_call | solution.py:361
  108.4 1.0 copy.6

commit v6 on v4

--- a/solution.py
+++ b/solution.py
@@ -12,7 +12,7 @@
 BF16 = jnp.bfloat16
 MESH = pl.DeviceIdType.MESH
 PIECES = 3
-EARLY = ((0, 512), (512, 896))
+EARLY = ((0, 768), (768, 1152))
 
 
 def kernel(dims, weight, len_ref, x_ref, g_ref, out_ref, xe, xv, xb, gv, xt, sendb, recvb, sendu, recvu, pre, fin, gin, gout,
@@ -124,14 +124,14 @@
 
     def gram(acc, block, new=False):
         nt = (((1,), (1,)), ((), ()))
-        left = lax.dot_general(block[:mid], block[:mid], nt, preferred_element_type=F32)
-        right = lax.dot_general(block, block[mid:], nt, preferred_element_type=F32)
+        top = lax.dot_general(block[:mid], block, nt, preferred_element_type=F32)
+        low = lax.dot_general(block[mid:], block[mid:], nt, preferred_element_type=F32)
         if new:
-            acc[:mid, :mid] = left
-            acc[:, mid:] = right
+            acc[:mid] = top
+            acc[mid:, mid:] = low
         else:
-            acc[:mid, :mid] += left
-            acc[:, mid:] += right
+            acc[:mid] += top
+            acc[mid:, mid:] += low
 
     x_copy.wait()
     gram(gin, xv[...], True)
@@ -139,15 +139,14 @@
         g_copy(h, 1).wait()
         gram(gout, gv[:seq, h * half:(h + 1) * half], h == 0)
 
-    row = lax.broadcasted_iota(jnp.int32, (seq, mid), 0)
-    col = lax.broadcasted_iota(jnp.int32, (seq, mid), 1)
+    row = lax.broadcasted_iota(jnp.int32, (mid, seq), 0)
+    col = lax.broadcasted_iota(jnp.int32, (mid, seq), 1)
     n_live = len_ref[0]
-    left_live = (row[:mid] < n_live) & (col[:mid] < n_live)
-    left = jnp.where(left_live, gin[:mid, :mid] * gout[:mid, :mid], 0.0)
-    twice = jnp.where(row < mid, 2.0, 1.0)
-    right_live = (row < n_live) & (col + mid < n_live)
-    right = jnp.where(right_live, gin[:, mid:] * gout[:, mid:] * twice, 0.0)
-    cells = left + right[:mid] + right[mid:]
+    twice = jnp.where(col >= mid, 2.0, 1.0)
+    top = jnp.where((row < n_live) & (col < n_live), gin[:mid] * gout[:mid] * twice, 0.0)
+    low_live = (row[:, mid:] + mid < n_live) & (col[:, mid:] < n_live)
+    low = jnp.where(low_live, gin[mid:, mid:] * gout[mid:, mid:], 0.0)
+    cells = top[:, :mid] + top[:, mid:] + low
     norm = jnp.sum(jnp.sum(cells, axis=0, keepdims=True), axis=1, keepdims=True)
     row_tile[...] = jnp.broadcast_to(norm, row_tile.shape)
 
@@ -190,6 +189,10 @@
         if j:
             col_copy(0, j, sec_y).start()
     cols_in[0, sec_y] = col_tile[...]
+    for k in (1, 2):
+        xb_swap(owner(k)).start()
+    for h in range(2):
+        g_swap(h, 0).start()
 
     len_swap.wait_recv()
     turn(first)
@@ -262,10 +265,6 @@
         part = jnp.dot(xt[first], gv[:, d * half + lo:d * half + hi], preferred_element_type=F32)
         sendb[d, 0, :, lo:hi] = part.astype(BF16)
         ring_copy(d, 0, 1).start()
-    for k in (1, 2):
-        xb_swap(owner(k)).start()
-    for h in range(2):
-        g_swap(h, 0).start()
     for d in range(2):
         up_copy(d).start()
 

time: 111 us -> 109 us (0.982)
  Pallas kernels: 109 us -> 107 us
    pallas_call x1, Pallas kernels: 109 us -> 107 us  [shards(): pl.pallas_call(functools.partial(kernel, (n_chips, side, rows), weight),...]
where the time goes in v6:
time: 109 us
  Pallas kernels  107 us (98%)
    pallas_call x1, Pallas kernels, shards(): pl.pallas_call(functools.partial(kernel, (n_chips, side, rows), weight),...  107 us

profile of v6, /device:TPU:1, one launch (start us, length us, event | category | flops | bytes accessed | tf_op | source)
XLA Modules:
  0.0 108.9 jit_solution(9432442885623695546)
XLA Ops:
  0.7 107.3 %shard_map.37 = bf16[128,4608]{1,0:T(8,128)(2,1)S(1)} custom-call(s32[1]{0:T(128)S(6)} %copy.5.len_ref, bf16[512,2048]{1,0:T(8,128)(2,1)} %bitcast.5, bf16[512,4608]{1,0:T(8,128)(2,1)} %bitcast.4), custom_call_target="tpu_custom_call" | custom-call | flops 13153337344 | bytes 6815744 | tf_op jit(solution)/shard_map/pallas_call | solution.py:362
  107.9 1.0 copy.6

commit v7 on v4

--- a/solution.py
+++ b/solution.py
@@ -12,7 +12,7 @@
 BF16 = jnp.bfloat16
 MESH = pl.DeviceIdType.MESH
 PIECES = 3
-EARLY = ((0, 512), (512, 896))
+EARLY = ((0, 512), (512, 1152))
 
 
 def kernel(dims, weight, len_ref, x_ref, g_ref, out_ref, xe, xv, xb, gv, xt, sendb, recvb, sendu, recvu, pre, fin, gin, gout,
@@ -135,6 +135,9 @@
 
     x_copy.wait()
     gram(gin, xv[...], True)
+    for p in range(1, len(EARLY)):
+        early_terms(p)
+        early_start(p)
     for h in range(2):
         g_copy(h, 1).wait()
         gram(gout, gv[:seq, h * half:(h + 1) * half], h == 0)
@@ -163,9 +166,6 @@
     for j in range(1, side):
         row_copy(j, sec_x).start()
     rows_in[sec_x] = row_tile[...]
-    for p in range(1, len(EARLY)):
-        early_terms(p)
-        early_start(p)
 
     token = lax.broadcasted_iota(jnp.int32, (seq, rows), 0).astype(F32)
 
@@ -190,6 +190,10 @@
         if j:
             col_copy(0, j, sec_y).start()
     cols_in[0, sec_y] = col_tile[...]
+    for k in (1, 2):
+        xb_swap(owner(k)).start()
+    for h in range(2):
+        g_swap(h, 0).start()
 
     len_swap.wait_recv()
     turn(first)
@@ -262,10 +266,6 @@
         part = jnp.dot(xt[first], gv[:, d * half + lo:d * half + hi], preferred_element_type=F32)
         sendb[d, 0, :, lo:hi] = part.astype(BF16)
         ring_copy(d, 0, 1).start()
-    for k in (1, 2):
-        xb_swap(owner(k)).start()
-    for h in range(2):
-        g_swap(h, 0).start()
     for d in range(2):
         up_copy(d).start()
 

time: 111 us -> 109 us (0.982)
  Pallas kernels: 109 us -> 107 us
    pallas_call x1, Pallas kernels: 109 us -> 107 us  [shards(): pl.pallas_call(functools.partial(kernel, (n_chips, side, rows), weight),...]
where the time goes in v7:
time: 109 us
  Pallas kernels  107 us (98%)
    pallas_call x1, Pallas kernels, shards(): pl.pallas_call(functools.partial(kernel, (n_chips, side, rows), weight),...  107 us

profile of v7, /device:TPU:1, one launch (start us, length us, event | category | flops | bytes accessed | tf_op | source)
XLA Modules:
  0.0 109.2 jit_solution(14794914385838330811)
XLA Ops:
  0.7 107.5 %shard_map.37 = bf16[128,4608]{1,0:T(8,128)(2,1)S(1)} custom-call(s32[1]{0:T(128)S(6)} %copy.5.len_ref, bf16[512,2048]{1,0:T(8,128)(2,1)} %bitcast.5, bf16[512,4608]{1,0:T(8,128)(2,1)} %bitcast.4), custom_call_target="tpu_custom_call" | custom-call | flops 13153337344 | bytes 6815744 | tf_op jit(solution)/shard_map/pallas_call | solution.py:363
  108.1 1.0 copy.6

commit v8 on v7

--- a/solution.py
+++ b/solution.py
@@ -51,15 +51,15 @@
     def x_cols(k, c):
         return pl.ds(pl.multiple_of((2 * k + c) * rows, 128), rows)
 
-    def g_cols(h, part):
-        return pl.ds(h * half + gone, half - gone) if part else pl.ds(h * half, gone)
+    def g_cols(h, part, cut):
+        return pl.ds(h * half + cut, half - cut) if part else pl.ds(h * half, cut)
 
     def g_copy(h, part):
-        cols = g_cols(h, part)
+        cols = g_cols(h, part, EARLY[0][1])
         return pltpu.make_async_copy(g_ref.at[:, cols], gv.at[pl.ds(0, seq), cols], g_sem.at[h, part])
 
     def g_swap(h, part):
-        cols = g_cols(h, part)
+        cols = g_cols(h, part, gone)
         return pltpu.make_async_remote_copy(
             g_ref.at[:, cols], gv.at[pl.ds(seq, seq), cols], g_send.at[h, part], g_recv.at[h, part],
             device_id=(partner, sec), device_id_type=MESH)
@@ -99,8 +99,8 @@
 
     def early_terms(p):
         for d in range(2):
-            if p == 0:
-                g_copy(d, 0).wait()
+            if p < 2:
+                g_copy(d, p).wait()
             lo, hi = EARLY[p]
             early = jnp.dot(xet, gv[:seq, d * half + lo:d * half + hi], preferred_element_type=F32).astype(BF16)
             for e in range(2):
@@ -117,10 +117,6 @@
     early_start(0)
     len_swap = pltpu.make_async_remote_copy(
         lens.at[0], lens.at[1], len_sem.at[0], len_sem.at[1], device_id=(partner, sec), device_id_type=MESH)
-    len_swap.start()
-    xb_swap(first).start()
-    for h in range(2):
-        g_swap(h, 1).start()
 
     def gram(acc, block, new=False):
         nt = (((1,), (1,)), ((), ()))
@@ -135,11 +131,14 @@
 
     x_copy.wait()
     gram(gin, xv[...], True)
+    len_swap.start()
+    xb_swap(first).start()
+    for h in range(2):
+        g_swap(h, 1).start()
     for p in range(1, len(EARLY)):
         early_terms(p)
         early_start(p)
     for h in range(2):
-        g_copy(h, 1).wait()
         gram(gout, gv[:seq, h * half:(h + 1) * half], h == 0)
 
     row = lax.broadcasted_iota(jnp.int32, (seq, mid), 0)
@@ -314,6 +313,26 @@
                 ring_copy(1 - d, steps - 2).wait_recv()
             fin[d * PIECES + s] = part + recvb[1 - d, steps - 2, :, cols(s)].astype(F32)
 
+    len_swap.wait_send()
+    for d in range(2):
+        up_copy(d).wait_send()
+        for e in range(2):
+            for p in range(len(EARLY)):
+                early_copy(d, p, e, e).wait_send()
+            g_swap(d, e).wait_send()
+        ring_copy(d, 0, 1).wait_send()
+        for i in range(steps - 1):
+            ring_copy(d, i).wait_send()
+    for j in range(side):
+        col_copy(1, j, sec_y).wait_send()
+        if j:
+            row_copy(j, sec_x).wait_send()
+            col_copy(0, j, sec_y).wait_send()
+
+    @pl.loop(0, n_chips)
+    def _(k):
+        xb_swap(k).wait_send()
+
     for s in range(PIECES):
         for d in range(2):
             c = d * PIECES + s
@@ -322,26 +341,9 @@
             done = (fin[c] + recvb[d, steps - 1, :, cols(s)].astype(F32)) * weight
             out_ref[:, cols(c)] = done.astype(out_ref.dtype)
 
-    len_swap.wait_send()
-    for d in range(2):
-        up_copy(d).wait_send()
-        for e in range(2):
-            for p in range(len(EARLY)):
-                early_copy(d, p, e, e).wait_send()
-            g_swap(d, e).wait_send()
-        for i in range(steps):
-            ring_copy(d, i).wait_send()
-        for i in (0, steps - 1):
-            ring_copy(d, i, 1).wait_send()
-    for j in range(side):
-        col_copy(1, j, sec_y).wait_send()
-        if j:
-            row_copy(j, sec_x).wait_send()
-            col_copy(0, j, sec_y).wait_send()
-
-    @pl.loop(0, n_chips)
-    def _(k):
-        xb_swap(k).wait_send()
+    for d in range(2):
+        for part in range(2):
+            ring_copy(d, steps - 1, part).wait_send()
 
 
 def shards(layer_inputs, output_grads, lengths):

time: 109 us -> 110 us (level)
  no operation moved by 1% of the time
where the time goes in v8:
time: 110 us
  Pallas kernels  108 us (98%)
    pallas_call x1, Pallas kernels, shards(): pl.pallas_call(functools.partial(kernel, (n_chips, side, rows), weight),...  108 us

profile of v8, /device:TPU:1, one launch (start us, length us, event | category | flops | bytes accessed | tf_op | source)
XLA Modules:
  0.0 109.8 jit_solution(5794373586869910444)
XLA Ops:
  0.7 108.1 %shard_map.37 = bf16[128,4608]{1,0:T(8,128)(2,1)S(1)} custom-call(s32[1]{0:T(128)S(6)} %copy.5.len_ref, bf16[512,2048]{1,0:T(8,128)(2,1)} %bitcast.5, bf16[512,4608]{1,0:T(8,128)(2,1)} %bitcast.4), custom_call_target="tpu_custom_call" | custom-call | flops 13153337344 | bytes 6815744 | tf_op jit(solution)/shard_map/pallas_call | solution.py:365
  108.8 1.0 copy.6

commit v9 on v8

--- a/solution.py
+++ b/solution.py
@@ -117,6 +117,10 @@
     early_start(0)
     len_swap = pltpu.make_async_remote_copy(
         lens.at[0], lens.at[1], len_sem.at[0], len_sem.at[1], device_id=(partner, sec), device_id_type=MESH)
+    len_swap.start()
+    xb_swap(first).start()
+    for h in range(2):
+        g_swap(h, 1).start()
 
     def gram(acc, block, new=False):
         nt = (((1,), (1,)), ((), ()))
@@ -131,10 +135,6 @@
 
     x_copy.wait()
     gram(gin, xv[...], True)
-    len_swap.start()
-    xb_swap(first).start()
-    for h in range(2):
-        g_swap(h, 1).start()
     for p in range(1, len(EARLY)):
         early_terms(p)
         early_start(p)

time: 110 us -> 110 us (level)
  no operation moved by 1% of the time
where the time goes in v9:
time: 110 us
  Pallas kernels  108 us (98%)
    pallas_call x1, Pallas kernels, shards(): pl.pallas_call(functools.partial(kernel, (n_chips, side, rows), weight),...  108 us

profile of v9, /device:TPU:1, one launch (start us, length us, event | category | flops | bytes accessed | tf_op | source)
XLA Modules:
  0.0 109.8 jit_solution(7186864548682022088)
XLA Ops:
  0.7 108.1 %shard_map.37 = bf16[128,4608]{1,0:T(8,128)(2,1)S(1)} custom-call(s32[1]{0:T(128)S(6)} %copy.5.len_ref, bf16[512,2048]{1,0:T(8,128)(2,1)} %bitcast.5, bf16[512,4608]{1,0:T(8,128)(2,1)} %bitcast.4), custom_call_target="tpu_custom_call" | custom-call | flops 13153337344 | bytes 6815744 | tf_op jit(solution)/shard_map/pallas_call | solution.py:365
  108.8 1.0 copy.6

commit v10 on v9

--- a/solution.py
+++ b/solution.py
@@ -12,7 +12,7 @@
 BF16 = jnp.bfloat16
 MESH = pl.DeviceIdType.MESH
 PIECES = 3
-EARLY = ((0, 512), (512, 1152))
+EARLY = ((0, 768), (768, 1152))
 
 
 def kernel(dims, weight, len_ref, x_ref, g_ref, out_ref, xe, xv, xb, gv, xt, sendb, recvb, sendu, recvu, pre, fin, gin, gout,
@@ -51,15 +51,15 @@
     def x_cols(k, c):
         return pl.ds(pl.multiple_of((2 * k + c) * rows, 128), rows)
 
-    def g_cols(h, part, cut):
-        return pl.ds(h * half + cut, half - cut) if part else pl.ds(h * half, cut)
+    def g_cols(h, part):
+        return pl.ds(h * half + gone, half - gone) if part else pl.ds(h * half, gone)
 
     def g_copy(h, part):
-        cols = g_cols(h, part, EARLY[0][1])
+        cols = g_cols(h, part)
         return pltpu.make_async_copy(g_ref.at[:, cols], gv.at[pl.ds(0, seq), cols], g_sem.at[h, part])
 
     def g_swap(h, part):
-        cols = g_cols(h, part, gone)
+        cols = g_cols(h, part)
         return pltpu.make_async_remote_copy(
             g_ref.at[:, cols], gv.at[pl.ds(seq, seq), cols], g_send.at[h, part], g_recv.at[h, part],
             device_id=(partner, sec), device_id_type=MESH)
@@ -99,8 +99,8 @@
 
     def early_terms(p):
         for d in range(2):
-            if p < 2:
-                g_copy(d, p).wait()
+            if p == 0:
+                g_copy(d, 0).wait()
             lo, hi = EARLY[p]
             early = jnp.dot(xet, gv[:seq, d * half + lo:d * half + hi], preferred_element_type=F32).astype(BF16)
             for e in range(2):
@@ -139,6 +139,7 @@
         early_terms(p)
         early_start(p)
     for h in range(2):
+        g_copy(h, 1).wait()
         gram(gout, gv[:seq, h * half:(h + 1) * half], h == 0)
 
     row = lax.broadcasted_iota(jnp.int32, (seq, mid), 0)

time: 110 us -> 109 us (level)
  no operation moved by 1% of the time
where the time goes in v10:
time: 109 us
  Pallas kernels  107 us (98%)
    pallas_call x1, Pallas kernels, shards(): pl.pallas_call(functools.partial(kernel, (n_chips, side, rows), weight),...  107 us

profile of v10, /device:TPU:1, one launch (start us, length us, event | category | flops | bytes accessed | tf_op | source)
XLA Modules:
  0.0 108.9 jit_solution(1654706191551272927)
XLA Ops:
  0.7 107.2 %shard_map.37 = bf16[128,4608]{1,0:T(8,128)(2,1)S(1)} custom-call(s32[1]{0:T(128)S(6)} %copy.5.len_ref, bf16[512,2048]{1,0:T(8,128)(2,1)} %bitcast.5, bf16[512,4608]{1,0:T(8,128)(2,1)} %bitcast.4), custom_call_target="tpu_custom_call" | custom-call | flops 13153337344 | bytes 6815744 | tf_op jit(solution)/shard_map/pallas_call | solution.py:366
  107.9 1.0 copy.6
